TPU v7x, 256 devices: a whole 4x4x8 slice. The times are simulated.
256 devices in a mesh: leaf: 64 (over z, x_lo, y), rhs: 4 (over x_hi, core).
Axes of the slice: x: 4 (x_hi: 2, x_lo: 2; x = x_hi * 2 + x_lo), y: 4, z: 8, core: 2. Of those that a mesh axis runs over, the one named last changes fastest.
Arguments:
- right_sides: bfloat16 [131072, 1536], P(('leaf', 'rhs')), may hold values from -6 to 6
- near_block: bfloat16 [131072, 2048], P('leaf'), may hold values from -0.125 to 0.125
- leaf_bases: bfloat16 [3, 131072, 128], P(None, 'leaf'), may hold values from -0.125 to 0.125
- couplings: float32 [3, 64, 128, 128], P(None, 'leaf'), may hold values from -0.5 to 0.5
- cluster_rows: int32 [64], P('leaf'), may hold values from 1 to 2048, 98304 in all
- nugget: float32 [131072], P(('leaf', 'rhs')), may hold values from 0.05 to 1
Outputs:
- product: bfloat16 [131072, 1536], P(('leaf', 'rhs'))
Inputs may be any that keep to these rules, and one draw needn't show every extreme that they name: `cluster_rows`: the largest cluster fills its whole slot.
All inputs are finite; a program needn't handle non-finite values. No bound on the sum of `cluster_rows` on one device may be relied on, other than what follows from the above.
Results may differ from a plain program's by a relative error of at most 0.0051.
Values may be sent and summed in bfloat16 or wider, within the bound.
A program may use at most 64 MiB of HBM per device.

v0:
```python
import jax
import jax.numpy as jnp
from jax import lax
from jax.sharding import PartitionSpec as P


def swapped(block, axis, apart):
    count = lax.axis_size(axis)
    route = []
    for low in range(count):
        high = low | 1 << apart
        if high != low and high < count:
            route += [(low, high), (high, low)]
    return lax.ppermute(block, axis, route)


def siblings_of(partial_sums):
    found = []
    for tree_level in range(3):
        running = partial_sums[tree_level]
        for bit_index in range(tree_level):
            running = running + swapped(running, "leaf", bit_index)
        found.append(swapped(running, "leaf", tree_level))
    return jnp.stack(found)


def far_terms(level_bases, couplings, partial_sums):
    sibling = siblings_of(partial_sums)
    mapped = jnp.einsum(
        "lrs,lsc->lrc", couplings[:, 0], sibling, precision=lax.Precision.HIGHEST
    ).astype(jnp.bfloat16)
    return jnp.einsum("lnr,lrc->nc", level_bases, mapped, preferred_element_type=jnp.float32)


def on_device(right_sides, near_block, leaf_bases, couplings, cluster_rows, nugget):
    quarter = right_sides.shape[0]
    leaf_rows = near_block.shape[0]
    row_count = cluster_rows[0]
    start_row = lax.axis_index("rhs") * quarter
    own_rows = start_row + jnp.arange(quarter, dtype=jnp.int32)
    own_valid = own_rows < row_count
    own_masked = jnp.where(own_valid[:, None], right_sides, jnp.zeros_like(right_sides))
    panel_cols = lax.all_to_all(own_masked, "rhs", split_axis=1, concat_axis=0, tiled=True)
    near_part = jnp.dot(near_block, panel_cols, preferred_element_type=jnp.float32)
    partial_sums = jnp.einsum(
        "lnr,nc->lrc", leaf_bases, panel_cols, preferred_element_type=jnp.float32
    )
    far_part = far_terms(leaf_bases, couplings, partial_sums)
    leaf_valid = jnp.arange(leaf_rows, dtype=jnp.int32) < row_count
    result_rows = jnp.where(leaf_valid[:, None], near_part + far_part, 0.0).astype(jnp.bfloat16)
    result_rows = lax.all_to_all(result_rows, "rhs", split_axis=0, concat_axis=1, tiled=True)
    result_rows = lax.optimization_barrier(result_rows)
    return (
        result_rows.astype(jnp.float32) + nugget[:, None] * own_masked.astype(jnp.float32)
    ).astype(jnp.bfloat16)


def solution(mesh):
    in_specs = (
        P(("leaf", "rhs"), None),
        P("leaf", None),
        P(None, "leaf", None),
        P(None, "leaf", None, None),
        P("leaf"),
        P(("leaf", "rhs")),
    )
    out_specs = P(("leaf", "rhs"), None)
    return jax.shard_map(
        on_device, mesh=mesh, in_specs=in_specs, out_specs=out_specs, check_vma=False
    )
```

profile of v0, /device:TPU:1, one launch (start us, length us, event | category | flops | bytes accessed | tf_op | source)
XLA Modules:
  0.0 97.2 jit_solution(11751050571351726046)
XLA Ops:
  0.8 1.6 %broadcast_select_fusion = bf16[512,1536]{1,0:T(8,128)(2,1)S(1)} fusion(bf16[512,1536]{1,0:T(8,128)(2,1)} %param.6, pred[512]{0:T(512)(128)(4,1)S(1)} %add_compare_fusion), kind=kLoop, calls=%fused_computation.5 | loop fusion | flops 786432 | bytes 3146240 | tf_op jit(solution)/shard_map/jit(_where)/select_n | solution.py:42
  2.4 1.6 %copy.9 = bf16[512,1536]{0,1:T(8,128)(2,1)} copy(bf16[512,1536]{1,0:T(8,128)(2,1)S(1)} %broadcast_select_fusion) | data formatting | bytes 3145728 | tf_op jit(solution)/shard_map/jit(_where)/select_n | solution.py:42
  4.0 27.3 %all_to_all.38 = bf16[512,4,384]{0,2,1:T(8,128)(2,1)S(1)} all-to-all(bf16[512,4,384]{0,2,1:T(8,128)(2,1)} %bitcast.51), channel_id=1, replica_groups=mesh['leaf'=64,'rhs'=4] {'rhs'}, dimensions={1} | all-to-all | bytes 3145728 | tf_op jit(solution)/shard_map/all_to_all | solution.py:43
  31.3 2.4 %copy.10 = bf16[4,512,384]{1,0,2:T(4,128)(2,1)} copy(bf16[4,512,384]{1,2,0:T(8,128)(2,1)S(1)} %bitcast.49) | data formatting | bytes 3145728 | tf_op jit(solution)/shard_map/all_to_all | solution.py:43
  33.6 3.9 %reshape.16 = bf16[2048,384,1]{0,1,2:T(8,128)(2,1)} reshape(bf16[4,512,384]{1,0,2:T(4,128)(2,1)} %copy.10) | data formatting | bytes 3145728 | tf_op jit(solution)/shard_map/all_to_all | solution.py:43
  37.5 2.4 %convolution_bitcast_fusion = f32[3,128,384]{1,2,0:T(8,128)S(1)} fusion(bf16[2048,384,1]{0,1,2:T(8,128)(2,1)} %reshape.16, bf16[3,2048,128]{2,1,0:T(8,128)(2,1)S(1)} %copy-done), kind=kOutput, calls=%fused_computation.6 | convolution fusion | flops 603979776 | bytes 3735552 | tf_op jit(solution)/shard_map/lnr,nc->lrc/dot_general | solution.py:45
  39.9 0.4 collective-permute-start.3
  40.3 1.1 %collective-permute-start.1 = (f32[128,384]{0,1:T(8,128)S(1)}, f32[128,384]{0,1:T(8,128)S(1)}, u32[]{:S(2)}, u32[]{:S(2)}) collective-permute-start(f32[128,384]{0,1:T(8,128)S(1)} %get-tuple-element.7), channel_id=1, source_target_pairs={{0,4},{4,0},{8,12},{12,8},{16,20},{20,16},{24,28},{28,24},{32,36},... | collective-permute-start | bytes 589832 | tf_op jit(solution)/shard_map/ppermute | solution.py:14
  41.5 3.9 %collective-permute-done.3 = f32[128,384]{0,1:T(8,128)S(1)} collective-permute-done((f32[128,384]{0,1:T(8,128)S(1)}, f32[128,384]{0,1:T(8,128)S(1)}, u32[]{:S(2)}, u32[]{:S(2)}) %collective-permute-start.3) | collective-permute-done | bytes 196640 | tf_op jit(solution)/shard_map/ppermute | solution.py:14
  45.4 4.2 %collective-permute-done.1 = f32[128,384]{0,1:T(8,128)S(1)} collective-permute-done((f32[128,384]{0,1:T(8,128)S(1)}, f32[128,384]{0,1:T(8,128)S(1)}, u32[]{:S(2)}, u32[]{:S(2)}) %collective-permute-start.1) | collective-permute-done | bytes 196640 | tf_op jit(solution)/shard_map/ppermute | solution.py:14
  49.6 2.0 %collective-permute-start.4 = (f32[128,384]{0,1:T(8,128)S(1)}, f32[128,384]{0,1:T(8,128)S(1)}, u32[]{:S(2)}, u32[]{:S(2)}) collective-permute-start(f32[128,384]{0,1:T(8,128)S(1)} %get-tuple-element.9), channel_id=1, source_target_pairs={{0,8},{8,0},{4,12},{12,4},{16,24},{24,16},{20,28},{28,20},{32,40},... | collective-permute-start | bytes 589832 | tf_op jit(solution)/shard_map/ppermute | solution.py:14
  51.7 0.4 collective-permute-start
  52.1 0.2 copy.14
  52.3 1.6 %collective-permute-start.2 = (f32[128,384]{0,1:T(8,128)S(1)}, f32[128,384]{0,1:T(8,128)S(1)}, u32[]{:S(2)}, u32[]{:S(2)}) collective-permute-start(f32[128,384]{0,1:T(8,128)S(1)} %get-tuple-element.8), channel_id=1, source_target_pairs={{0,8},{8,0},{4,12},{12,4},{16,24},{24,16},{20,28},{28,20},{32,40},... | collective-permute-start | bytes 589832 | tf_op jit(solution)/shard_map/ppermute | solution.py:14
  53.9 1.8 %collective-permute-done.4 = f32[128,384]{0,1:T(8,128)S(1)} collective-permute-done((f32[128,384]{0,1:T(8,128)S(1)}, f32[128,384]{0,1:T(8,128)S(1)}, u32[]{:S(2)}, u32[]{:S(2)}) %collective-permute-start.4) | collective-permute-done | bytes 196640 | tf_op jit(solution)/shard_map/ppermute | solution.py:14
  55.8 0.1 collective-permute-start.5
  55.9 5.9 %fusion.12 = f32[384,2048]{1,0:T(8,128)S(1)} fusion(bf16[2048,384]{0,1:T(8,128)(2,1)S(1)} %bitcast.55, bf16[2048,2048]{1,0:T(8,128)(2,1)} %param.7), kind=kOutput, calls=%fused_computation.23 | convolution fusion | flops 3221225472 | bytes 13107200 | tf_op jit(solution)/shard_map/dot_general | solution.py:44
  61.8 2.0 %collective-permute-done.2 = f32[128,384]{0,1:T(8,128)S(1)} collective-permute-done((f32[128,384]{0,1:T(8,128)S(1)}, f32[128,384]{0,1:T(8,128)S(1)}, u32[]{:S(2)}, u32[]{:S(2)}) %collective-permute-start.2) | collective-permute-done | bytes 196640 | tf_op jit(solution)/shard_map/ppermute | solution.py:14
  63.8 0.6 fusion.2
  64.4 1.0 %fusion.1 = bf16[384,2048]{1,0:T(8,128)(2,1)S(1)} fusion(f32[384,2048]{1,0:T(8,128)S(1)} %fusion.12, bf16[3,128,384]{1,2,0:T(8,128)(2,1)S(1)} %fusion.2, bf16[3,2048,128]{2,1,0:T(8,128)(2,1)S(1)} %copy-done, pred[2048]{0:T(1024)(128)(4,1)S(1)} %iota_compare_fusion), kind=kOutput, calls=%fused_computation.2 | convolution fusion | flops 606339072 | bytes 6588416 | tf_op jit(solution)/shard_map/lnr,lrc->nc/dot_general | solution.py:32
  65.5 0.1 copy.16
  65.6 26.3 %all_to_all.39 = bf16[4,512,384]{1,2,0:T(8,128)(2,1)S(1)} all-to-all(bf16[4,512,384]{1,2,0:T(8,128)(2,1)S(1)} %bitcast.52), channel_id=1, replica_groups=mesh['leaf'=64,'rhs'=4] {'rhs'}, dimensions={0} | all-to-all | bytes 3145728 | tf_op jit(solution)/shard_map/all_to_all | solution.py:51
  92.0 1.6 %copy.12 = bf16[512,1536]{1,0:T(8,128)(2,1)} copy(bf16[512,1536]{0,1:T(8,128)(2,1)S(1)} %bitcast.53) | data formatting | bytes 3145728 | tf_op jit(solution)/shard_map/optimization_barrier | solution.py:52
  93.5 3.7 %add_convert_fusion = bf16[512,1536]{1,0:T(8,128)(2,1)} fusion(bf16[512,1536]{1,0:T(8,128)(2,1)} %copy.12, f32[512]{0:T(512)S(1)} %copy-done.2, bf16[512,1536]{1,0:T(8,128)(2,1)} %param.6, pred[512]{0:T(512)(128)(4,1)S(1)} %add_compare_fusion), kind=kLoop, calls=%fused_computation.3 | loop fusion | flops 4718592 | bytes 4721152 | tf_op jit(solution)/shard_map/convert_element_type | solution.py:55
  (13 shorter events, 0.2 us)
Async XLA Ops:
  0.0 37.5 %copy-start = (bf16[3,2048,128]{2,1,0:T(8,128)(2,1)S(1)}, bf16[3,2048,128]{2,1,0:T(8,128)(2,1)}, u32[]{:S(2)}) copy-start(bf16[3,2048,128]{2,1,0:T(8,128)(2,1)} %param.8) | copy-start | bytes 4718596
  39.9 5.4 %collective-permute-start.3 = (f32[128,384]{0,1:T(8,128)S(1)}, f32[128,384]{0,1:T(8,128)S(1)}, u32[]{:S(2)}, u32[]{:S(2)}) collective-permute-start(f32[128,384]{0,1:T(8,128)S(1)} %get-tuple-element.6), channel_id=1, source_target_pairs={{0,4},{4,0},{8,12},{12,8},{16,20},{20,16},{24,28},{28,24},{32,36},... | collective-permute-start | bytes 589832 | tf_op jit(solution)/shard_map/ppermute | solution.py:14
  40.3 9.2 %collective-permute-start.1 = (f32[128,384]{0,1:T(8,128)S(1)}, f32[128,384]{0,1:T(8,128)S(1)}, u32[]{:S(2)}, u32[]{:S(2)}) collective-permute-start(f32[128,384]{0,1:T(8,128)S(1)} %get-tuple-element.7), channel_id=1, source_target_pairs={{0,4},{4,0},{8,12},{12,8},{16,20},{20,16},{24,28},{28,24},{32,36},... | collective-permute-start | bytes 589832 | tf_op jit(solution)/shard_map/ppermute | solution.py:14
  49.6 6.1 %collective-permute-start.4 = (f32[128,384]{0,1:T(8,128)S(1)}, f32[128,384]{0,1:T(8,128)S(1)}, u32[]{:S(2)}, u32[]{:S(2)}) collective-permute-start(f32[128,384]{0,1:T(8,128)S(1)} %get-tuple-element.9), channel_id=1, source_target_pairs={{0,8},{8,0},{4,12},{12,4},{16,24},{24,16},{20,28},{28,20},{32,40},... | collective-permute-start | bytes 589832 | tf_op jit(solution)/shard_map/ppermute | solution.py:14
  51.7 10.1 %collective-permute-start = (f32[128,384]{0,1:T(8,128)S(1)}, f32[128,384]{0,1:T(8,128)S(1)}, u32[]{:S(2)}, u32[]{:S(2)}) collective-permute-start(f32[128,384]{0,1:T(8,128)S(1)} %get-tuple-element.5), channel_id=1, source_target_pairs={{0,4},{4,0},{8,12},{12,8},{16,20},{20,16},{24,28},{28,24},{32,36},... | collective-permute-start | bytes 589832 | tf_op jit(solution)/shard_map/ppermute | solution.py:14
  52.3 11.5 %collective-permute-start.2 = (f32[128,384]{0,1:T(8,128)S(1)}, f32[128,384]{0,1:T(8,128)S(1)}, u32[]{:S(2)}, u32[]{:S(2)}) collective-permute-start(f32[128,384]{0,1:T(8,128)S(1)} %get-tuple-element.8), channel_id=1, source_target_pairs={{0,8},{8,0},{4,12},{12,4},{16,24},{24,16},{20,28},{28,20},{32,40},... | collective-permute-start | bytes 589832 | tf_op jit(solution)/shard_map/ppermute | solution.py:14
  55.8 8.0 %collective-permute-start.5 = (f32[128,384]{0,1:T(8,128)S(1)}, f32[128,384]{0,1:T(8,128)S(1)}, u32[]{:S(2)}, u32[]{:S(2)}) collective-permute-start(f32[128,384]{0,1:T(8,128)S(1)} %add.30), channel_id=1, source_target_pairs={{0,16},{16,0},{4,20},{20,4},{8,24},{24,8},{12,28},{28,12},{32,48},... | collective-permute-start | bytes 589832 | tf_op jit(solution)/shard_map/ppermute | solution.py:14
  55.9 7.9 %copy-start.1 = (f32[3,1,128,128]{3,2,1,0:T(8,128)S(1)}, f32[3,1,128,128]{3,2,1,0:T(8,128)}, u32[]{:S(2)}) copy-start(f32[3,1,128,128]{3,2,1,0:T(8,128)} %param.9) | copy-start | bytes 589828
  92.0 1.6 %copy-start.2 = (f32[512]{0:T(512)S(1)}, f32[512]{0:T(512)}, u32[]{:S(2)}) copy-start(f32[512]{0:T(512)} %param.11) | copy-start | bytes 6148
where the time goes:
time: 97.5 us; the launch traced here: 97.2 us
  blocking collectives  53.6 us (55%)
  waiting for transfers between devices  11.9 us (12%)
  matrix products  9.95 us (10%)
  local copies, waits for them, and re-layouts  9.76 us (10%)
  starting transfers between devices  5.72 us (6%)
  other arithmetic  5.36 us (5%)
    all_to_all x1, blocking collectives, on_device(): lax.all_to_all(own_masked, 'rhs', split_axis=1, concat_axis=0, tiled=True)  27.3 us
    all_to_all x1, blocking collectives, on_device(): lax.all_to_all(result_rows, 'rhs', split_axis=0, concat_axis=1, tiled=True)  26.3 us
    ppermute x6, waiting for transfers between devices, swapped(): return lax.ppermute(block, axis, route)  11.9 us
    all_to_all x3, local copies, waits for them, and re-layouts, on_device(): lax.all_to_all(own_masked, 'rhs', split_axis=1, concat_axis=0, tiled=True)  6.42 us
    dot_general x1, matrix products, on_device(): jnp.dot(near_block, panel_cols, preferred_element_type=jnp.float32)  5.91 us
    ppermute x6, starting transfers between devices, swapped(): return lax.ppermute(block, axis, route)  5.72 us
    convert_element_type x1, other arithmetic, on_device(): return (result_rows.astype(jnp.float32) + nugget[:, None] * own_masked.as...  3.68 us
    dot_general x1, matrix products, on_device(): jnp.einsum('lnr,nc->lrc', leaf_bases, panel_cols, preferred_element_type=...  2.38 us
  transfers between devices with their start and end apart: 6, of which 4 were waited for; matrix products, arithmetic and copies ran while one was open for 6% of the time, Pallas kernels for 0%

commit v1 on v0

v1 whole, which is shorter than its diff:
```python
import jax
import jax.numpy as jnp
from jax import lax
from jax.experimental import pallas as pl
from jax.experimental.pallas import tpu as pltpu
from jax.sharding import PartitionSpec as P

MESH = pl.DeviceIdType.MESH
BF16 = jnp.bfloat16
F32 = jnp.float32

LEAF = 2048
OWN = 512
PANEL = 384
PIECE = 128
PIECES = 3
RANK = 128
LEVELS = 3
PART = 32
BLOCK = 512


def kernel(
    x_hbm, near_hbm, bases_hbm, core_hbm, rows_smem, op_hbm,
    xs, relay, near, bases, bases_t, core, mask, total, result, back,
    out1, in1, sum2, out2, in2, sib2,
    local_sem, send_sem, recv_sem,
):
    leaf = lax.axis_index("leaf")
    rhs = lax.axis_index("rhs")
    y = leaf % 4
    x_lo = (leaf // 4) % 2
    panel = (rhs + 2 * x_lo) % 4
    mate = rhs + 1 - 2 * (rhs % 2)
    far = (rhs + 2) % 4
    mate_panel = panel + 1 - 2 * (panel % 2)
    far_panel = (panel + 2) % 4
    cross_panel = 3 - panel
    ys = (y + 1 - 2 * (y % 2), (y + 2) % 4, 3 - y)
    to_mate = (leaf, mate)
    to_far = (leaf, far)
    to_ys = tuple((leaf - y + other, rhs) for other in ys)
    to_pair = (leaf + 4 - 8 * x_lo, far)

    barrier = pltpu.get_barrier_semaphore()
    for device in (to_mate, to_far, *to_ys, to_pair):
        pl.semaphore_signal(barrier, inc=1, device_id=device, device_id_type=MESH)

    def rows_of(index):
        return pl.ds(pl.multiple_of(index * OWN, OWN), OWN)

    def cols_of(which, k):
        return pl.ds(pl.multiple_of(which * PANEL + k * PIECE, PIECE), PIECE)

    local = []

    def load(src, dst):
        copy = pltpu.make_async_copy(src, dst, local_sem.at[len(local)])
        copy.start()
        local.append(copy)
        return copy

    own_x = [load(x_hbm.at[:, cols_of(panel, k)], xs.at[k, rows_of(rhs)]) for k in range(PIECES)]
    load_bases = [
        load(bases_hbm.at[l], bases.at[:, pl.ds(l * RANK, RANK)]) for l in range(LEVELS)
    ]
    load_core = load(core_hbm, core)
    load_near = load(near_hbm, near)

    def remote(index, src, dst, device):
        return pltpu.make_async_remote_copy(
            src_ref=src, dst_ref=dst, send_sem=send_sem.at[index], recv_sem=recv_sem.at[index],
            device_id=device, device_id_type=MESH,
        )

    def copies(k):
        base = 15 * k
        c = {}
        c["relay"] = remote(base, x_hbm.at[:, cols_of(cross_panel, k)], relay.at[k], to_mate)
        c["mate"] = remote(
            base + 1, x_hbm.at[:, cols_of(mate_panel, k)], xs.at[k, rows_of(rhs)], to_mate
        )
        c["far"] = remote(
            base + 2, x_hbm.at[:, cols_of(far_panel, k)], xs.at[k, rows_of(rhs)], to_far
        )
        c["on"] = remote(base + 3, relay.at[k], xs.at[k, rows_of(mate)], to_far)
        c["one"] = [
            remote(base + 4 + j, out1.at[k, j], in1.at[k, j], to_ys[j]) for j in range(3)
        ]
        c["two"] = remote(base + 7, out2.at[k], in2.at[k], to_pair)
        mine = sib2.at[k, pl.ds(pl.multiple_of(y * PART, PART), PART)]
        c["three"] = [remote(base + 8 + j, in2.at[k], mine, to_ys[j]) for j in range(3)]
        c["back"] = remote(base + 11, result.at[k, rows_of(3 - rhs)], back.at[k], to_mate)
        c["rmate"] = remote(
            base + 12, result.at[k, rows_of(mate)], op_hbm.at[:, cols_of(panel, k)], to_mate
        )
        c["rfar"] = remote(
            base + 13, result.at[k, rows_of(far)], op_hbm.at[:, cols_of(panel, k)], to_far
        )
        c["ron"] = remote(
            base + 14, back.at[k], op_hbm.at[:, cols_of(mate_panel, k)], to_far
        )
        c["rown"] = pltpu.make_async_copy(
            result.at[k, rows_of(rhs)], op_hbm.at[:, cols_of(panel, k)], local_sem.at[8 + k]
        )
        return c

    every = [copies(k) for k in range(PIECES)]

    pl.semaphore_wait(barrier, 6)

    every[0]["relay"].start()
    every[0]["far"].start()
    every[1]["relay"].start()
    every[0]["mate"].start()
    every[2]["relay"].start()
    every[1]["mate"].start()
    every[2]["mate"].start()
    for k in range(PIECES):
        every[k]["relay"].wait_recv()
        every[k]["on"].start()
        if k + 1 < PIECES:
            every[k + 1]["far"].start()

    count = rows_smem[0]

    def make_mask(i, carry):
        at = pl.ds(pl.multiple_of(i * BLOCK, BLOCK), BLOCK)
        row = lax.broadcasted_iota(jnp.int32, (BLOCK, PIECE), 0) + i * BLOCK
        mask[at, :] = jnp.where(row < count, 1.0, 0.0).astype(BF16)
        return carry

    lax.fori_loop(0, LEAF // BLOCK, make_mask, 0)

    for copy in load_bases:
        copy.wait()
    for i in range(LEAF // BLOCK):
        at = pl.ds(i * BLOCK, BLOCK)
        bases_t[:, at] = bases[at, :].T

    def gather(k):
        c = every[k]
        own_x[k].wait()
        c["mate"].wait_recv()
        c["far"].wait_recv()
        c["on"].wait_recv()
        xs[k] = xs[k] * mask[...]
        part = jnp.dot(bases_t[...], xs[k], preferred_element_type=F32)
        sum2[k] = part[2 * RANK :]
        out1[k, 0, :RANK] = part[:RANK].astype(BF16)
        middle = part[RANK : 2 * RANK].astype(BF16)
        out1[k, 1, :RANK] = middle
        out1[k, 2, :RANK] = middle
        for j in range(3):
            at = pl.ds(pl.multiple_of(ys[j] * PART, PART), PART)
            out1[k, j, RANK:] = sum2[k, at].astype(BF16)
            c["one"][j].start()

    def near_field(k):
        def step(i, carry):
            at = pl.ds(pl.multiple_of(i * BLOCK, BLOCK), BLOCK)
            total[at, :] = jnp.dot(near[at, :], xs[k], preferred_element_type=F32)
            return carry

        lax.fori_loop(0, LEAF // BLOCK, step, 0)

    def exchange(k):
        c = every[k]
        for copy in c["one"]:
            copy.wait_recv()
        at = pl.ds(pl.multiple_of(y * PART, PART), PART)
        part = sum2[k, at]
        for j in range(3):
            part = part + in1[k, j, RANK:].astype(F32)
        out2[k] = part
        c["two"].start()

    def spread(k):
        c = every[k]
        c["two"].wait_recv()
        for copy in c["three"]:
            copy.start()

    def finish(k):
        c = every[k]
        at = pl.ds(pl.multiple_of(y * PART, PART), PART)
        sib2[k, at] = in2[k]
        for copy in c["three"]:
            copy.wait_recv()
        sibling = (
            in1[k, 0, :RANK].astype(F32),
            in1[k, 1, :RANK].astype(F32) + in1[k, 2, :RANK].astype(F32),
            sib2[k],
        )
        mapped = jnp.concatenate(
            [
                jnp.dot(
                    core[l, 0], sibling[l], precision=lax.Precision.HIGHEST,
                    preferred_element_type=F32,
                ).astype(BF16)
                for l in range(LEVELS)
            ],
            axis=0,
        )

        def step(i, carry):
            at = pl.ds(pl.multiple_of(i * BLOCK, BLOCK), BLOCK)
            value = total[at, :] + jnp.dot(bases[at, :], mapped, preferred_element_type=F32)
            result[k, at, :] = (value * mask[at, :].astype(F32)).astype(BF16)
            return carry

        lax.fori_loop(0, LEAF // BLOCK, step, 0)
        c["back"].start()
        c["rfar"].start()
        c["rmate"].start()
        c["rown"].start()

    def relay_back(k):
        every[k]["back"].wait_recv()
        every[k]["ron"].start()

    gather(0)
    load_near.wait()
    load_core.wait()
    near_field(0)
    exchange(0)
    spread(0)
    gather(1)
    finish(0)
    near_field(1)
    relay_back(0)
    exchange(1)
    spread(1)
    gather(2)
    finish(1)
    near_field(2)
    relay_back(1)
    exchange(2)
    spread(2)
    finish(2)
    relay_back(2)

    for k in range(PIECES):
        c = every[k]
        c["rown"].wait()
        for name in ("relay", "mate", "far", "on", "two", "back", "rmate", "rfar", "ron"):
            c[name].wait_send()
        for copy in c["one"] + c["three"]:
            copy.wait_send()
        for name in ("rmate", "rfar", "ron"):
            c[name].wait_recv()


def operator(right_sides, near_block, leaf_bases, couplings, cluster_rows):
    hbm = pl.BlockSpec(memory_space=pltpu.HBM)
    dma = pltpu.SemaphoreType.DMA
    return pl.pallas_call(
        kernel,
        out_shape=jax.ShapeDtypeStruct(right_sides.shape, BF16),
        in_specs=[hbm, hbm, hbm, hbm, pl.BlockSpec(memory_space=pltpu.SMEM)],
        out_specs=hbm,
        scratch_shapes=[
            pltpu.VMEM((PIECES, LEAF, PIECE), BF16),
            pltpu.VMEM((PIECES, OWN, PIECE), BF16),
            pltpu.VMEM((LEAF, LEAF), BF16),
            pltpu.VMEM((LEAF, LEVELS * RANK), BF16),
            pltpu.VMEM((LEVELS * RANK, LEAF), BF16),
            pltpu.VMEM((LEVELS, 1, RANK, RANK), F32),
            pltpu.VMEM((LEAF, PIECE), BF16),
            pltpu.VMEM((LEAF, PIECE), F32),
            pltpu.VMEM((PIECES, LEAF, PIECE), BF16),
            pltpu.VMEM((PIECES, OWN, PIECE), BF16),
            pltpu.VMEM((PIECES, 3, RANK + PART, PIECE), BF16),
            pltpu.VMEM((PIECES, 3, RANK + PART, PIECE), BF16),
            pltpu.VMEM((PIECES, RANK, PIECE), F32),
            pltpu.VMEM((PIECES, PART, PIECE), F32),
            pltpu.VMEM((PIECES, PART, PIECE), F32),
            pltpu.VMEM((PIECES, RANK, PIECE), F32),
            dma((11,)),
            dma((15 * PIECES,)),
            dma((15 * PIECES,)),
        ],
        compiler_params=pltpu.CompilerParams(
            collective_id=0, has_side_effects=True, vmem_limit_bytes=48 << 20
        ),
        cost_estimate=pl.CostEstimate(
            flops=4 * 10**9, bytes_accessed=15 * 10**6, transcendentals=0
        ),
        name="operator",
    )(right_sides, near_block, leaf_bases, couplings, cluster_rows)


def on_device(right_sides, near_block, leaf_bases, couplings, cluster_rows, nugget):
    rows = operator(right_sides, near_block, leaf_bases, couplings, cluster_rows)
    row = lax.axis_index("rhs") * OWN + jnp.arange(OWN, dtype=jnp.int32)
    masked = jnp.where((row < cluster_rows[0])[:, None], right_sides, jnp.zeros_like(right_sides))
    return (rows.astype(F32) + nugget[:, None] * masked.astype(F32)).astype(BF16)


def solution(mesh):
    in_specs = (
        P(("leaf", "rhs"), None),
        P("leaf", None),
        P(None, "leaf", None),
        P(None, "leaf", None, None),
        P("leaf"),
        P(("leaf", "rhs")),
    )
    return jax.shard_map(
        on_device, mesh=mesh, in_specs=in_specs, out_specs=P(("leaf", "rhs"), None), check_vma=False
    )
```

time: 97.5 us -> 70.6 us (0.72)
  Pallas kernels: 0 us -> 64.2 us
  blocking collectives: 53.6 us -> 0 us
  waiting for transfers between devices: 11.9 us -> 0 us
  matrix products: 9.95 us -> 0 us
  local copies, waits for them, and re-layouts: 9.76 us -> 3.74 us
  starting transfers between devices: 5.72 us -> 0 us
  other arithmetic: 5.36 us -> 1.81 us
    pallas_call x0 -> x1, Pallas kernels: none -> 64.2 us  [operator(): pl.pallas_call(kernel, out_shape=jax.ShapeDtypeStruct(right_sides.shape,...]
    all_to_all x2 -> x0, blocking collectives: 53.6 us -> none  [the longest x1 27.3 us: on_device(): lax.all_to_all(own_masked, 'rhs', split_axis=1, concat_axis=0, tiled=True)]
    ppermute x6 -> x0, waiting for transfers between devices: 11.9 us -> none  [swapped(): return lax.ppermute(block, axis, route)]
    dot_general x4 -> x0, matrix products: 9.95 us -> none  [the longest x1 5.91 us: on_device(): jnp.dot(near_block, panel_cols, preferred_element_type=jnp.float32)]
    all_to_all x4 -> x0, local copies, waits for them, and re-layouts: 6.56 us -> none  [the longest x3 6.42 us: on_device(): lax.all_to_all(own_masked, 'rhs', split_axis=1, concat_axis=0, tiled=True)]
    ppermute x6 -> x0, starting transfers between devices: 5.72 us -> none  [swapped(): return lax.ppermute(block, axis, route)]
    unnamed x6 -> x8, local copies, waits for them, and re-layouts: 0.01 us -> 3.74 us
    convert_element_type x1, other arithmetic: 3.68 us -> 1.8 us  [on_device(): (rows.astype(F32) + nugget[:, None] * masked.astype(F32)).astype(BF16)]
  transfers between devices with their start and end apart: 6 -> 0, of which waited for: 4 -> 0; matrix products, arithmetic and copies ran while one was open for 6% -> 0% of each run, Pallas kernels for 0% -> 0%
where the time goes in v1:
time: 70.6 us; the launch traced here: 70.4 us
  Pallas kernels  64.2 us (91%)
  local copies, waits for them, and re-layouts  3.74 us (5%)
  other arithmetic  1.81 us (3%)
    pallas_call x1, Pallas kernels, operator(): pl.pallas_call(kernel, out_shape=jax.ShapeDtypeStruct(right_sides.shape,...  64.2 us
    unnamed x8, local copies, waits for them, and re-layouts  3.74 us
    convert_element_type x1, other arithmetic, on_device(): (rows.astype(F32) + nugget[:, None] * masked.astype(F32)).astype(BF16)  1.8 us

profile of v1, /device:TPU:1, one launch (start us, length us, event | category | flops | bytes accessed | tf_op | source)
XLA Modules:
  0.0 70.4 jit_solution(7861697312305424831)
XLA Ops:
  0.7 0.0 copy-start
  0.7 1.4 %copy-done = bf16[512,1536]{1,0:T(8,128)(2,1)S(1)} copy-done((bf16[512,1536]{1,0:T(8,128)(2,1)S(1)}, bf16[512,1536]{1,0:T(8,128)(2,1)}, u32[]{:S(2)}) %copy-start) | copy-done | bytes 1572888
  2.1 0.0 copy-start.1
  2.1 1.4 %copy-done.1 = bf16[3,2048,128]{2,1,0:T(8,128)(2,1)S(1)} copy-done((bf16[3,2048,128]{2,1,0:T(8,128)(2,1)S(1)}, bf16[3,2048,128]{2,1,0:T(8,128)(2,1)}, u32[]{:S(2)}) %copy-start.1) | copy-done | bytes 1572888
  3.5 0.0 copy-start.2
  3.5 0.9 %copy-done.2 = f32[3,1,128,128]{3,2,1,0:T(8,128)S(1)} copy-done((f32[3,1,128,128]{3,2,1,0:T(8,128)S(1)}, f32[3,1,128,128]{3,2,1,0:T(8,128)}, u32[]{:S(2)}) %copy-start.2) | copy-done | bytes 196632
  4.4 0.0 copy-start.3
  4.4 64.2 %operator.1 = bf16[512,1536]{1,0:T(8,128)(2,1)S(1)} custom-call(bf16[512,1536]{1,0:T(8,128)(2,1)S(1)} %copy-done, bf16[2048,2048]{1,0:T(8,128)(2,1)} %near_hbm.1, bf16[3,2048,128]{2,1,0:T(8,128)(2,1)S(1)} %copy-done.1, f32[3,1,128,128]{3,2,1,0:T(8,128)S(1)} %copy-done.2, s32[1]{0:T(128)} %copy.7.rows_smem), custom_call_target="tpu_custom_call" | custom-call | flops 4000000000 | bytes 15000000 | tf_op jit(solution)/shard_map/operator/pallas_call | solution.py:257
  68.6 0.0 copy-done.3
  68.6 1.8 %add_convert_fusion = bf16[512,1536]{1,0:T(8,128)(2,1)} fusion(bf16[512,1536]{1,0:T(8,128)(2,1)S(1)} %operator.1, bf16[512,1536]{1,0:T(8,128)(2,1)S(1)} %copy-done, f32[512]{0:T(512)S(1)} %copy-done.3, pred[512]{0:T(512)(128)(4,1)S(1)} %add_compare_fusion), kind=kLoop, calls=%fused_computation | loop fusion | flops 4718592 | bytes 4721152 | tf_op jit(solution)/shard_map/convert_element_type | solution.py:297
  (1 shorter events, 0.0 us)
Async XLA Ops:
  0.7 1.4 %copy-start = (bf16[512,1536]{1,0:T(8,128)(2,1)S(1)}, bf16[512,1536]{1,0:T(8,128)(2,1)}, u32[]{:S(2)}) copy-start(bf16[512,1536]{1,0:T(8,128)(2,1)} %x_hbm.1) | copy-start | bytes 4718596
  2.1 1.4 %copy-start.1 = (bf16[3,2048,128]{2,1,0:T(8,128)(2,1)S(1)}, bf16[3,2048,128]{2,1,0:T(8,128)(2,1)}, u32[]{:S(2)}) copy-start(bf16[3,2048,128]{2,1,0:T(8,128)(2,1)} %bases_hbm.1) | copy-start | bytes 4718596
  3.5 0.9 %copy-start.2 = (f32[3,1,128,128]{3,2,1,0:T(8,128)S(1)}, f32[3,1,128,128]{3,2,1,0:T(8,128)}, u32[]{:S(2)}) copy-start(f32[3,1,128,128]{3,2,1,0:T(8,128)} %core_hbm.1) | copy-start | bytes 589828
  4.4 64.2 %copy-start.3 = (f32[512]{0:T(512)S(1)}, f32[512]{0:T(512)}, u32[]{:S(2)}) copy-start(f32[512]{0:T(512)} %param.11) | copy-start | bytes 6148

commit v2 on v1

v2 whole, which is shorter than its diff:
```python
import jax
import jax.numpy as jnp
from jax import lax
from jax.experimental import pallas as pl
from jax.experimental.pallas import tpu as pltpu
from jax.sharding import PartitionSpec as P

MESH = pl.DeviceIdType.MESH
BF16 = jnp.bfloat16
F32 = jnp.float32

LEAF = 2048
CHIP = 1024
OWN = 512
PIECE = 128
SENT = 2
KEPT = 2
PIECES = SENT + KEPT
PANEL = SENT * PIECE
KEPT_AT = 4 * PANEL
RANK = 128
LEVELS = 3
PART = 32
BLOCK = 512
LAST = PIECES - 1
COPIES = 18


def kernel(
    x_hbm, near_hbm, bases_hbm, core_hbm, rows_hbm, op_hbm,
    xs, relay, xm, near, bases, bases_t, core, rows, mask, total, result, back,
    out0, in0, out1, in1, sum2, out2, in2, sib2, in3,
    local_sem, send_sem, recv_sem,
):
    leaf = lax.axis_index("leaf")
    rhs = lax.axis_index("rhs")
    y = leaf % 4
    x_lo = (leaf // 4) % 2
    mate = rhs + 1 - 2 * (rhs % 2)
    far = (rhs + 2) % 4
    cross = 3 - rhs
    ys = (y + 1 - 2 * (y % 2), (y + 2) % 4, 3 - y)
    to_mate = (leaf, mate)
    to_far = (leaf, far)
    to_ys = tuple((leaf - y + other, rhs) for other in ys)
    to_pair = (leaf + 4 - 8 * x_lo, rhs)

    barrier = pltpu.get_barrier_semaphore()
    for device in (to_far, to_pair, *to_ys, to_mate):
        pl.semaphore_signal(barrier, inc=1, device_id=device, device_id_type=MESH)

    def rows_of(index):
        return pl.ds(pl.multiple_of(index * OWN, OWN), OWN)

    def cols_of(which, k):
        if k < SENT:
            at = which * PANEL + k * PIECE
        else:
            at = KEPT_AT + (which % 2) * KEPT * PIECE + (k - SENT) * PIECE
        return pl.ds(pl.multiple_of(at, PIECE), PIECE)

    def part_of(index):
        return pl.ds(pl.multiple_of(index * PART, PART), PART)

    local = []

    def load(src, dst):
        copy = pltpu.make_async_copy(src, dst, local_sem.at[len(local)])
        copy.start()
        local.append(copy)
        return copy

    load_rows = load(rows_hbm, rows)
    load_bases = [
        load(bases_hbm.at[l], bases.at[:, pl.ds(l * RANK, RANK)]) for l in range(LEVELS)
    ]

    def remote(index, src, dst, device):
        return pltpu.make_async_remote_copy(
            src_ref=src, dst_ref=dst, send_sem=send_sem.at[index], recv_sem=recv_sem.at[index],
            device_id=device, device_id_type=MESH,
        )

    def copies(k):
        at = COPIES * k
        c = {}
        if k < SENT:
            c["relay"] = remote(at, x_hbm.at[:, cols_of(cross, k)], relay.at[k], to_mate)
            passed = relay.at[k]
        else:
            passed = xs.at[k, rows_of(mate)]
        c["mate"] = remote(at + 1, x_hbm.at[:, cols_of(mate, k)], xs.at[k, rows_of(rhs)], to_mate)
        c["far"] = remote(at + 2, x_hbm.at[:, cols_of(far, k)], xs.at[k, rows_of(rhs)], to_far)
        c["on"] = remote(at + 3, passed, xs.at[k, rows_of(mate)], to_far)
        c["zero"] = [remote(at + 4 + j, out0.at[k, j], in0.at[k, j], to_ys[j]) for j in range(3)]
        if k < LAST:
            first = pl.ds(0, PART)
            c["one"] = [
                remote(at + 7 + j, out1.at[k, j], in1.at[k, j], to_ys[j]) for j in range(3)
            ]
            c["two"] = remote(at + 10, out2.at[k, first], in2.at[k, first], to_pair)
            c["three"] = [
                remote(at + 11 + j, in2.at[k, first], sib2.at[k, part_of(y)], to_ys[j])
                for j in range(3)
            ]
        else:
            c["two"] = remote(at + 10, out2.at[k], in2.at[k], to_pair)
            c["three"] = [remote(at + 11 + j, in2.at[k], in3.at[j], to_ys[j]) for j in range(3)]
        mine = op_hbm.at[:, cols_of(rhs, k)]
        if k < SENT:
            c["rfar"] = remote(at + 14, result.at[k, rows_of(far)], mine, to_far)
            c["back"] = remote(at + 15, result.at[k, rows_of(cross)], back.at[k], to_mate)
            c["ron"] = remote(at + 17, back.at[k], op_hbm.at[:, cols_of(mate, k)], to_far)
        c["rmate"] = remote(at + 16, result.at[k, rows_of(mate)], mine, to_mate)
        c["rown"] = pltpu.make_async_copy(result.at[k, rows_of(rhs)], mine, local_sem.at[10 + k])
        return c

    every = [copies(k) for k in range(PIECES)]

    pl.semaphore_wait(barrier, 6)

    every[0]["far"].start()
    for k in range(SENT):
        every[k]["relay"].start()
    for k in range(PIECES):
        every[k]["mate"].start()
    own_x = [load(x_hbm.at[:, cols_of(rhs, k)], xs.at[k, rows_of(rhs)]) for k in range(PIECES)]
    load_near = load(near_hbm, near)
    load_core = load(core_hbm, core)
    for k in range(SENT):
        every[k]["relay"].wait_recv()
        if k:
            every[k]["far"].start()
        every[k]["on"].start()
    every[2]["far"].start()

    load_rows.wait()
    count = rows[0]

    def make_mask(i, carry):
        at = pl.ds(pl.multiple_of(i * BLOCK, BLOCK), BLOCK)
        row = lax.broadcasted_iota(jnp.int32, (BLOCK, PIECE), 0) + i * BLOCK
        mask[at, :] = jnp.where(row < count, 1.0, 0.0).astype(BF16)
        return carry

    lax.fori_loop(0, LEAF // BLOCK, make_mask, 0)

    for copy in load_bases:
        copy.wait()

    def transpose(i, carry):
        at = pl.ds(pl.multiple_of(i * PIECE, PIECE), PIECE)
        for l in range(LEVELS):
            level = pl.ds(l * RANK, RANK)
            bases_t[level, at] = (bases[at, level] * mask[at, :]).T
        return carry

    lax.fori_loop(0, LEAF // PIECE, transpose, 0)

    def gather(k):
        c = every[k]
        own_x[k].wait()
        if k < SENT:
            c["mate"].wait_recv()
        c["far"].wait_recv()
        c["on"].wait_recv()
        part = jnp.dot(bases_t[...], xs[k], preferred_element_type=F32)
        if k < LAST:
            sum2[k] = part[2 * RANK :]
            for j in range(3):
                out1[k, j] = sum2[k, part_of(ys[j])].astype(BF16)
                c["one"][j].start()
        else:
            out2[k] = part[2 * RANK :].astype(BF16)
            c["two"].start()
        middle = part[RANK : 2 * RANK].astype(BF16)
        out0[k, 0] = part[:RANK].astype(BF16)
        out0[k, 1] = middle
        out0[k, 2] = middle
        for copy in c["zero"]:
            copy.start()

    def near_field(k):
        xm[...] = xs[k] * mask[...]
        if k < SENT:
            for i in range(LEAF // CHIP):
                at = pl.ds(i * CHIP, CHIP)
                total[k, at] = jnp.dot(near[at, :], xm[...], preferred_element_type=F32)
        else:
            at = pl.ds(pl.multiple_of((rhs // 2) * CHIP, CHIP), CHIP)
            total[k, at] = jnp.dot(near[at, :], xm[...], preferred_element_type=F32)

    def exchange(k):
        c = every[k]
        part = sum2[k, part_of(y)]
        for j in range(3):
            c["one"][j].wait_recv()
            part = part + in1[k, j].astype(F32)
        out2[k, :PART] = part.astype(BF16)
        c["two"].start()

    def spread(k):
        c = every[k]
        c["two"].wait_recv()
        for copy in c["three"]:
            copy.start()
        if k < LAST:
            sib2[k, part_of(y)] = in2[k, :PART]

    def finish(k):
        c = every[k]
        for copy in c["zero"] + c["three"]:
            copy.wait_recv()
        if k < LAST:
            top = sib2[k].astype(F32)
        else:
            top = in2[k].astype(F32)
            for j in range(3):
                top = top + in3[j].astype(F32)
        sibling = (
            in0[k, 0].astype(F32),
            in0[k, 1].astype(F32) + in0[k, 2].astype(F32),
            top,
        )
        mapped = jnp.concatenate(
            [
                jnp.dot(
                    core[l, 0], sibling[l], precision=lax.Precision.HIGHEST,
                    preferred_element_type=F32,
                ).astype(BF16)
                for l in range(LEVELS)
            ],
            axis=0,
        )
        owners = ((mate, "rmate"), (rhs, "rown"))
        if k < SENT:
            owners = ((far, "rfar"), (cross, "back")) + owners
        for owner, name in owners:
            at = rows_of(owner)
            value = total[k, at] + jnp.dot(bases[at, :], mapped, preferred_element_type=F32)
            result[k, at, :] = value.astype(BF16)
            c[name].start()

    gather(0)
    load_near.wait()
    load_core.wait()
    near_field(0)
    exchange(0)
    every[2]["mate"].wait_recv()
    every[2]["on"].start()
    every[3]["far"].start()
    gather(1)
    near_field(1)
    spread(0)
    exchange(1)
    every[3]["mate"].wait_recv()
    every[3]["on"].start()
    gather(2)
    near_field(2)
    finish(0)
    spread(1)
    exchange(2)
    gather(3)
    every[0]["back"].wait_recv()
    every[0]["ron"].start()
    near_field(3)
    finish(1)
    spread(2)
    every[1]["back"].wait_recv()
    every[1]["ron"].start()
    spread(3)
    finish(2)
    finish(3)

    for k in range(PIECES):
        c = every[k]
        c["rown"].wait()
        for name in ("relay", "mate", "far", "on", "two", "rfar", "back", "rmate", "ron"):
            if name in c:
                c[name].wait_send()
        for copy in c["zero"] + c.get("one", []) + c["three"]:
            copy.wait_send()
        for name in ("rmate", "rfar", "ron"):
            if name in c:
                c[name].wait_recv()


def operator(right_sides, near_block, leaf_bases, couplings, cluster_rows):
    hbm = pl.BlockSpec(memory_space=pltpu.HBM)
    dma = pltpu.SemaphoreType.DMA
    return pl.pallas_call(
        kernel,
        out_shape=jax.ShapeDtypeStruct(right_sides.shape, BF16),
        in_specs=[hbm] * 5,
        out_specs=hbm,
        scratch_shapes=[
            pltpu.VMEM((PIECES, LEAF, PIECE), BF16),
            pltpu.VMEM((SENT, OWN, PIECE), BF16),
            pltpu.VMEM((LEAF, PIECE), BF16),
            pltpu.VMEM((LEAF, LEAF), BF16),
            pltpu.VMEM((LEAF, LEVELS * RANK), BF16),
            pltpu.VMEM((LEVELS * RANK, LEAF), BF16),
            pltpu.VMEM((LEVELS, 1, RANK, RANK), F32),
            pltpu.SMEM((1,), jnp.int32),
            pltpu.VMEM((LEAF, PIECE), BF16),
            pltpu.VMEM((PIECES, LEAF, PIECE), F32),
            pltpu.VMEM((PIECES, LEAF, PIECE), BF16),
            pltpu.VMEM((SENT, OWN, PIECE), BF16),
            pltpu.VMEM((PIECES, 3, RANK, PIECE), BF16),
            pltpu.VMEM((PIECES, 3, RANK, PIECE), BF16),
            pltpu.VMEM((LAST, 3, PART, PIECE), BF16),
            pltpu.VMEM((LAST, 3, PART, PIECE), BF16),
            pltpu.VMEM((LAST, RANK, PIECE), F32),
            pltpu.VMEM((PIECES, RANK, PIECE), BF16),
            pltpu.VMEM((PIECES, RANK, PIECE), BF16),
            pltpu.VMEM((LAST, RANK, PIECE), BF16),
            pltpu.VMEM((3, RANK, PIECE), BF16),
            dma((10 + PIECES,)),
            dma((COPIES * PIECES,)),
            dma((COPIES * PIECES,)),
        ],
        compiler_params=pltpu.CompilerParams(
            collective_id=0, has_side_effects=True, vmem_limit_bytes=60 << 20
        ),
        cost_estimate=pl.CostEstimate(
            flops=4 * 10**9, bytes_accessed=15 * 10**6, transcendentals=0
        ),
        name="operator",
    )(right_sides, near_block, leaf_bases, couplings, cluster_rows)


def on_device(right_sides, near_block, leaf_bases, couplings, cluster_rows, nugget):
    rows = operator(right_sides, near_block, leaf_bases, couplings, cluster_rows)
    row = lax.axis_index("rhs") * OWN + jnp.arange(OWN, dtype=jnp.int32)
    value = rows.astype(F32) + nugget[:, None] * right_sides.astype(F32)
    return jnp.where((row < cluster_rows[0])[:, None], value, 0.0).astype(BF16)


def solution(mesh):
    in_specs = (
        P(("leaf", "rhs"), None),
        P("leaf", None),
        P(None, "leaf", None),
        P(None, "leaf", None, None),
        P("leaf"),
        P(("leaf", "rhs")),
    )
    return jax.shard_map(
        on_device, mesh=mesh, in_specs=in_specs, out_specs=P(("leaf", "rhs"), None), check_vma=False
    )
```

time: 70.6 us -> 48.5 us (0.69)
  Pallas kernels: 64.2 us -> 44.5 us
  local copies, waits for them, and re-layouts: 3.74 us -> 0.01 us
  other arithmetic: 1.81 us -> 3.19 us
    pallas_call x1, Pallas kernels: 64.2 us -> 44.5 us  [operator(): pl.pallas_call(kernel, out_shape=jax.ShapeDtypeStruct(right_sides.shape,...]
    unnamed x8 -> x4, local copies, waits for them, and re-layouts: 3.74 us -> 0.01 us
    convert_element_type x1, other arithmetic: 1.8 us -> 3.19 us  [on_device(): return jnp.where((row < cluster_rows[0])[:, None], value, 0.0).astype(BF16)]
where the time goes in v2:
time: 48.5 us; the launch traced here: 48.4 us
  Pallas kernels  44.5 us (92%)
  other arithmetic  3.19 us (7%)
  between operations  0.7 us (1%)
    pallas_call x1, Pallas kernels, operator(): pl.pallas_call(kernel, out_shape=jax.ShapeDtypeStruct(right_sides.shape,...  44.5 us
    convert_element_type x1, other arithmetic, on_device(): return jnp.where((row < cluster_rows[0])[:, None], value, 0.0).astype(BF16)  3.19 us

profile of v2, /device:TPU:1, one launch (start us, length us, event | category | flops | bytes accessed | tf_op | source)
XLA Modules:
  0.0 48.4 jit_solution(8780565049230401852)
XLA Ops:
  0.7 0.0 copy-start
  0.7 0.0 copy-start.1
  0.7 44.5 %operator.1 = bf16[512,1536]{1,0:T(8,128)(2,1)} custom-call(bf16[512,1536]{1,0:T(8,128)(2,1)} %x_hbm.1, bf16[2048,2048]{1,0:T(8,128)(2,1)} %near_hbm.1, bf16[3,2048,128]{2,1,0:T(8,128)(2,1)} %bases_hbm.1, f32[3,1,128,128]{3,2,1,0:T(8,128)} %core_hbm.1, s32[1]{0:T(128)} %copy.7.rows_hbm), custom_call_target="tpu_custom_call" | custom-call | flops 4000000000 | bytes 15000000 | tf_op jit(solution)/shard_map/operator/pallas_call | solution.py:291
  45.2 0.0 copy-done
  45.2 0.0 copy-done.1
  45.2 3.2 %select_convert_fusion = bf16[512,1536]{1,0:T(8,128)(2,1)} fusion(bf16[512,1536]{1,0:T(8,128)(2,1)S(1)} %copy-done, bf16[512,1536]{1,0:T(8,128)(2,1)} %operator.1, f32[512]{0:T(512)S(1)} %copy-done.1, pred[512]{0:T(512)(128)(4,1)S(1)} %add_compare_fusion), kind=kLoop, calls=%fused_computation | loop fusion | flops 4718592 | bytes 4721152 | tf_op jit(solution)/shard_map/convert_element_type | solution.py:336
  (1 shorter events, 0.0 us)
Async XLA Ops:
  0.7 44.5 %copy-start = (bf16[512,1536]{1,0:T(8,128)(2,1)S(1)}, bf16[512,1536]{1,0:T(8,128)(2,1)}, u32[]{:S(2)}) copy-start(bf16[512,1536]{1,0:T(8,128)(2,1)} %x_hbm.1) | copy-start | bytes 4718596
  0.7 44.5 %copy-start.1 = (f32[512]{0:T(512)S(1)}, f32[512]{0:T(512)}, u32[]{:S(2)}) copy-start(f32[512]{0:T(512)} %param.11) | copy-start | bytes 6148

commit v3 on v2

--- a/solution.py
+++ b/solution.py
@@ -20,6 +20,7 @@
 KEPT_AT = 4 * PANEL
 RANK = 128
 LEVELS = 3
+RHS = 1536
 PART = 32
 BLOCK = 512
 LAST = PIECES - 1
@@ -27,8 +28,8 @@
 
 
 def kernel(
-    x_hbm, near_hbm, bases_hbm, core_hbm, rows_hbm, op_hbm,
-    xs, relay, xm, near, bases, bases_t, core, rows, mask, total, result, back,
+    x_hbm, near_hbm, bases_hbm, core_hbm, rows_hbm, nugget_hbm, out,
+    own, noise, scale, live, xs, relay, xm, near, bases, bases_t, core, rows, mask, total, result, back,
     out0, in0, out1, in1, sum2, out2, in2, sib2, in3,
     local_sem, send_sem, recv_sem,
 ):
@@ -71,6 +72,7 @@
         return copy
 
     load_rows = load(rows_hbm, rows)
+    load_noise = load(nugget_hbm, noise)
     load_bases = [
         load(bases_hbm.at[l], bases.at[:, pl.ds(l * RANK, RANK)]) for l in range(LEVELS)
     ]
@@ -106,13 +108,12 @@
         else:
             c["two"] = remote(at + 10, out2.at[k], in2.at[k], to_pair)
             c["three"] = [remote(at + 11 + j, in2.at[k], in3.at[j], to_ys[j]) for j in range(3)]
-        mine = op_hbm.at[:, cols_of(rhs, k)]
+        mine = out.at[:, cols_of(rhs, k)]
         if k < SENT:
             c["rfar"] = remote(at + 14, result.at[k, rows_of(far)], mine, to_far)
             c["back"] = remote(at + 15, result.at[k, rows_of(cross)], back.at[k], to_mate)
-            c["ron"] = remote(at + 17, back.at[k], op_hbm.at[:, cols_of(mate, k)], to_far)
+            c["ron"] = remote(at + 17, back.at[k], out.at[:, cols_of(mate, k)], to_far)
         c["rmate"] = remote(at + 16, result.at[k, rows_of(mate)], mine, to_mate)
-        c["rown"] = pltpu.make_async_copy(result.at[k, rows_of(rhs)], mine, local_sem.at[10 + k])
         return c
 
     every = [copies(k) for k in range(PIECES)]
@@ -127,6 +128,7 @@
     own_x = [load(x_hbm.at[:, cols_of(rhs, k)], xs.at[k, rows_of(rhs)]) for k in range(PIECES)]
     load_near = load(near_hbm, near)
     load_core = load(core_hbm, core)
+    load_own = load(x_hbm, own)
     for k in range(SENT):
         every[k]["relay"].wait_recv()
         if k:
@@ -156,6 +158,24 @@
         return carry
 
     lax.fori_loop(0, LEAF // PIECE, transpose, 0)
+
+    load_noise.wait()
+    for i in range(OWN // PIECE):
+        at = pl.ds(i * PIECE, PIECE)
+        spread_out = jnp.broadcast_to(noise[at].reshape(1, PIECE), (PIECE, PIECE)).T
+        alive = mask[pl.ds(pl.multiple_of(rhs * OWN + i * PIECE, PIECE), PIECE), :].astype(F32)
+        live[at, :] = alive
+        scale[at, :] = spread_out * alive
+
+    def add_noise(cols, value):
+        out[:, cols] = (
+            value.astype(F32) * live[...] + scale[...] * own[:, cols].astype(F32)
+        ).astype(BF16)
+
+    def settle(k, name, which):
+        every[k][name].wait_recv()
+        cols = cols_of(which, k)
+        add_noise(cols, out[:, cols])
 
     def gather(k):
         c = every[k]
@@ -232,7 +252,7 @@
             ],
             axis=0,
         )
-        owners = ((mate, "rmate"), (rhs, "rown"))
+        owners = ((mate, "rmate"),)
         if k < SENT:
             owners = ((far, "rfar"), (cross, "back")) + owners
         for owner, name in owners:
@@ -240,10 +260,14 @@
             value = total[k, at] + jnp.dot(bases[at, :], mapped, preferred_element_type=F32)
             result[k, at, :] = value.astype(BF16)
             c[name].start()
+        at = rows_of(rhs)
+        value = total[k, at] + jnp.dot(bases[at, :], mapped, preferred_element_type=F32)
+        add_noise(cols_of(rhs, k), value.astype(BF16))
 
     gather(0)
     load_near.wait()
     load_core.wait()
+    load_own.wait()
     near_field(0)
     exchange(0)
     every[2]["mate"].wait_recv()
@@ -268,32 +292,40 @@
     spread(2)
     every[1]["back"].wait_recv()
     every[1]["ron"].start()
+    settle(0, "rmate", mate)
+    settle(1, "rmate", mate)
     spread(3)
+    settle(0, "rfar", far)
     finish(2)
+    settle(0, "ron", cross)
     finish(3)
+    settle(2, "rmate", mate)
+    settle(1, "rfar", far)
+    settle(3, "rmate", mate)
+    settle(1, "ron", cross)
 
     for k in range(PIECES):
         c = every[k]
-        c["rown"].wait()
         for name in ("relay", "mate", "far", "on", "two", "rfar", "back", "rmate", "ron"):
             if name in c:
                 c[name].wait_send()
         for copy in c["zero"] + c.get("one", []) + c["three"]:
             copy.wait_send()
-        for name in ("rmate", "rfar", "ron"):
-            if name in c:
-                c[name].wait_recv()
-
-
-def operator(right_sides, near_block, leaf_bases, couplings, cluster_rows):
+
+
+def on_device(*arrays):
     hbm = pl.BlockSpec(memory_space=pltpu.HBM)
     dma = pltpu.SemaphoreType.DMA
     return pl.pallas_call(
         kernel,
-        out_shape=jax.ShapeDtypeStruct(right_sides.shape, BF16),
-        in_specs=[hbm] * 5,
-        out_specs=hbm,
+        out_shape=pltpu.VMEM((OWN, RHS), BF16),
+        in_specs=[hbm] * 6,
+        out_specs=pl.BlockSpec(memory_space=pltpu.VMEM),
         scratch_shapes=[
+            pltpu.VMEM((OWN, RHS), BF16),
+            pltpu.VMEM((OWN,), F32),
+            pltpu.VMEM((OWN, PIECE), F32),
+            pltpu.VMEM((OWN, PIECE), F32),
             pltpu.VMEM((PIECES, LEAF, PIECE), BF16),
             pltpu.VMEM((SENT, OWN, PIECE), BF16),
             pltpu.VMEM((LEAF, PIECE), BF16),
@@ -315,25 +347,22 @@
             pltpu.VMEM((PIECES, RANK, PIECE), BF16),
             pltpu.VMEM((LAST, RANK, PIECE), BF16),
             pltpu.VMEM((3, RANK, PIECE), BF16),
-            dma((10 + PIECES,)),
+            dma((12,)),
             dma((COPIES * PIECES,)),
             dma((COPIES * PIECES,)),
         ],
         compiler_params=pltpu.CompilerParams(
-            collective_id=0, has_side_effects=True, vmem_limit_bytes=60 << 20
+            collective_id=0, has_side_effects=True, vmem_limit_bytes=48 << 20
         ),
         cost_estimate=pl.CostEstimate(
             flops=4 * 10**9, bytes_accessed=15 * 10**6, transcendentals=0
         ),
         name="operator",
-    )(right_sides, near_block, leaf_bases, couplings, cluster_rows)
-
-
-def on_device(right_sides, near_block, leaf_bases, couplings, cluster_rows, nugget):
-    rows = operator(right_sides, near_block, leaf_bases, couplings, cluster_rows)
-    row = lax.axis_index("rhs") * OWN + jnp.arange(OWN, dtype=jnp.int32)
-    value = rows.astype(F32) + nugget[:, None] * right_sides.astype(F32)
-    return jnp.where((row < cluster_rows[0])[:, None], value, 0.0).astype(BF16)
+    )(
+        *(pltpu.with_memory_space_constraint(array, pltpu.HBM) for array in arrays[:4]),
+        arrays[4],
+        pltpu.with_memory_space_constraint(arrays[5], pltpu.HBM),
+    )
 
 
 def solution(mesh):

time: 48.5 us -> 46.3 us (0.955)
  other arithmetic: 3.19 us -> 0 us
  local copies, waits for them, and re-layouts: 0.01 us -> 1.15 us
    convert_element_type x1 -> x0, other arithmetic: 3.19 us -> none  [on_device(): return jnp.where((row < cluster_rows[0])[:, None], value, 0.0).astype(BF16)]
    unnamed x4 -> x1, local copies, waits for them, and re-layouts: 0.01 us -> 1.15 us
where the time goes in v3:
time: 46.3 us; the launch traced here: 46.2 us
  Pallas kernels  44.4 us (96%)
  local copies, waits for them, and re-layouts  1.15 us (2%)
  between operations  0.66 us (1%)
    pallas_call x1, Pallas kernels, on_device(): pl.pallas_call(kernel, out_shape=pltpu.VMEM((OWN, RHS), BF16), in_specs=[...  44.4 us
    unnamed x1, local copies, waits for them, and re-layouts  1.15 us

profile of v3, /device:TPU:1, one launch (start us, length us, event | category | flops | bytes accessed | tf_op | source)
XLA Modules:
  0.0 46.2 jit_solution(7628941177997870303)
XLA Ops:
  0.7 44.4 %operator.1 = bf16[512,1536]{1,0:T(8,128)(2,1)S(1)} custom-call(bf16[512,1536]{1,0:T(8,128)(2,1)} %x_hbm.1, bf16[2048,2048]{1,0:T(8,128)(2,1)} %near_hbm.1, bf16[3,2048,128]{2,1,0:T(8,128)(2,1)} %bases_hbm.1, f32[3,1,128,128]{3,2,1,0:T(8,128)} %core_hbm.1, s32[1]{0:T(128)S(6)} %copy.9.rows_hbm, f32[512]{0:T(512)} %nugget_hbm.1), custom_call_target="tpu_custom_call" | custom-call | flops 4000000000 | bytes 15000000 | tf_op jit(solution)/shard_map/operator/pallas_call | solution.py:319
  45.1 1.1 %copy.8 = bf16[512,1536]{1,0:T(8,128)(2,1)} copy(bf16[512,1536]{1,0:T(8,128)(2,1)S(1)} %operator.1) | data formatting | bytes 3145728

commit v4 on v3

--- a/solution.py
+++ b/solution.py
@@ -23,13 +23,13 @@
 RHS = 1536
 PART = 32
 BLOCK = 512
-LAST = PIECES - 1
+CROSS = (3,)
 COPIES = 18
 
 
 def kernel(
-    x_hbm, near_hbm, bases_hbm, core_hbm, rows_hbm, nugget_hbm, out,
-    own, noise, scale, live, xs, relay, xm, near, bases, bases_t, core, rows, mask, total, result, back,
+    x_hbm, near_hbm, bases_hbm, core_hbm, rows, nugget_hbm, out,
+    own, noise, scale, live, xs, relay, xm, near, bases, bases_t, core, mask, total, total_kept, result, back,
     out0, in0, out1, in1, sum2, out2, in2, sib2, in3,
     local_sem, send_sem, recv_sem,
 ):
@@ -71,7 +71,6 @@
         local.append(copy)
         return copy
 
-    load_rows = load(rows_hbm, rows)
     load_noise = load(nugget_hbm, noise)
     load_bases = [
         load(bases_hbm.at[l], bases.at[:, pl.ds(l * RANK, RANK)]) for l in range(LEVELS)
@@ -95,7 +94,7 @@
         c["far"] = remote(at + 2, x_hbm.at[:, cols_of(far, k)], xs.at[k, rows_of(rhs)], to_far)
         c["on"] = remote(at + 3, passed, xs.at[k, rows_of(mate)], to_far)
         c["zero"] = [remote(at + 4 + j, out0.at[k, j], in0.at[k, j], to_ys[j]) for j in range(3)]
-        if k < LAST:
+        if k not in CROSS:
             first = pl.ds(0, PART)
             c["one"] = [
                 remote(at + 7 + j, out1.at[k, j], in1.at[k, j], to_ys[j]) for j in range(3)
@@ -107,7 +106,7 @@
             ]
         else:
             c["two"] = remote(at + 10, out2.at[k], in2.at[k], to_pair)
-            c["three"] = [remote(at + 11 + j, in2.at[k], in3.at[j], to_ys[j]) for j in range(3)]
+            c["three"] = [remote(at + 11 + j, in2.at[k], in3.at[k, j], to_ys[j]) for j in range(3)]
         mine = out.at[:, cols_of(rhs, k)]
         if k < SENT:
             c["rfar"] = remote(at + 14, result.at[k, rows_of(far)], mine, to_far)
@@ -120,24 +119,17 @@
 
     pl.semaphore_wait(barrier, 6)
 
+    every[0]["relay"].start()
     every[0]["far"].start()
-    for k in range(SENT):
-        every[k]["relay"].start()
-    for k in range(PIECES):
+    every[1]["relay"].start()
+    every[0]["mate"].start()
+    every[0]["relay"].wait_recv()
+    every[0]["on"].start()
+    own_x = [load(x_hbm.at[:, cols_of(rhs, k)], xs.at[k, rows_of(rhs)]) for k in range(PIECES)]
+    for k in range(1, PIECES):
         every[k]["mate"].start()
-    own_x = [load(x_hbm.at[:, cols_of(rhs, k)], xs.at[k, rows_of(rhs)]) for k in range(PIECES)]
-    load_near = load(near_hbm, near)
-    load_core = load(core_hbm, core)
-    load_own = load(x_hbm, own)
-    for k in range(SENT):
-        every[k]["relay"].wait_recv()
-        if k:
-            every[k]["far"].start()
-        every[k]["on"].start()
-    every[2]["far"].start()
-
-    load_rows.wait()
-    count = rows[0]
+
+    count = rows[0:1, :]
 
     def make_mask(i, carry):
         at = pl.ds(pl.multiple_of(i * BLOCK, BLOCK), BLOCK)
@@ -158,6 +150,14 @@
         return carry
 
     lax.fori_loop(0, LEAF // PIECE, transpose, 0)
+
+    every[1]["relay"].wait_recv()
+    every[1]["far"].start()
+    every[1]["on"].start()
+    every[2]["far"].start()
+    load_near = load(near_hbm, near)
+    load_core = load(core_hbm, core)
+    load_own = load(x_hbm, own)
 
     load_noise.wait()
     for i in range(OWN // PIECE):
@@ -185,7 +185,7 @@
         c["far"].wait_recv()
         c["on"].wait_recv()
         part = jnp.dot(bases_t[...], xs[k], preferred_element_type=F32)
-        if k < LAST:
+        if k not in CROSS:
             sum2[k] = part[2 * RANK :]
             for j in range(3):
                 out1[k, j] = sum2[k, part_of(ys[j])].astype(BF16)
@@ -200,15 +200,24 @@
         for copy in c["zero"]:
             copy.start()
 
-    def near_field(k):
-        xm[...] = xs[k] * mask[...]
-        if k < SENT:
-            for i in range(LEAF // CHIP):
-                at = pl.ds(i * CHIP, CHIP)
-                total[k, at] = jnp.dot(near[at, :], xm[...], preferred_element_type=F32)
-        else:
-            at = pl.ds(pl.multiple_of((rhs // 2) * CHIP, CHIP), CHIP)
-            total[k, at] = jnp.dot(near[at, :], xm[...], preferred_element_type=F32)
+    def near_sent(half):
+        if half == 0:
+            for k in range(SENT):
+                xm[:, k * PIECE : (k + 1) * PIECE] = xs[k] * mask[...]
+        at = pl.ds(half * CHIP, CHIP)
+        total[at, :] = jnp.dot(near[at, :], xm[...], preferred_element_type=F32)
+
+    def near_kept():
+        for k in range(KEPT):
+            xm[:, k * PIECE : (k + 1) * PIECE] = xs[SENT + k] * mask[...]
+        at = pl.ds(pl.multiple_of((rhs // 2) * CHIP, CHIP), CHIP)
+        total_kept[...] = jnp.dot(near[at, :], xm[...], preferred_element_type=F32)
+
+    def near_of(k, owner):
+        if k < SENT:
+            return total[rows_of(owner), k * PIECE : (k + 1) * PIECE]
+        at = (k - SENT) * PIECE
+        return total_kept[rows_of(owner % 2), at : at + PIECE]
 
     def exchange(k):
         c = every[k]
@@ -224,19 +233,19 @@
         c["two"].wait_recv()
         for copy in c["three"]:
             copy.start()
-        if k < LAST:
+        if k not in CROSS:
             sib2[k, part_of(y)] = in2[k, :PART]
 
     def finish(k):
         c = every[k]
         for copy in c["zero"] + c["three"]:
             copy.wait_recv()
-        if k < LAST:
+        if k not in CROSS:
             top = sib2[k].astype(F32)
         else:
             top = in2[k].astype(F32)
             for j in range(3):
-                top = top + in3[j].astype(F32)
+                top = top + in3[k, j].astype(F32)
         sibling = (
             in0[k, 0].astype(F32),
             in0[k, 1].astype(F32) + in0[k, 2].astype(F32),
@@ -257,44 +266,45 @@
             owners = ((far, "rfar"), (cross, "back")) + owners
         for owner, name in owners:
             at = rows_of(owner)
-            value = total[k, at] + jnp.dot(bases[at, :], mapped, preferred_element_type=F32)
+            value = near_of(k, owner) + jnp.dot(
+                bases[at, :], mapped, preferred_element_type=F32
+            )
             result[k, at, :] = value.astype(BF16)
             c[name].start()
         at = rows_of(rhs)
-        value = total[k, at] + jnp.dot(bases[at, :], mapped, preferred_element_type=F32)
+        value = near_of(k, rhs) + jnp.dot(bases[at, :], mapped, preferred_element_type=F32)
         add_noise(cols_of(rhs, k), value.astype(BF16))
 
     gather(0)
     load_near.wait()
     load_core.wait()
     load_own.wait()
-    near_field(0)
     exchange(0)
     every[2]["mate"].wait_recv()
     every[2]["on"].start()
     every[3]["far"].start()
     gather(1)
-    near_field(1)
     spread(0)
+    near_sent(0)
+    near_sent(1)
     exchange(1)
     every[3]["mate"].wait_recv()
     every[3]["on"].start()
     gather(2)
-    near_field(2)
     finish(0)
     spread(1)
     exchange(2)
     gather(3)
     every[0]["back"].wait_recv()
     every[0]["ron"].start()
-    near_field(3)
     finish(1)
     spread(2)
     every[1]["back"].wait_recv()
     every[1]["ron"].start()
+    spread(3)
+    near_kept()
     settle(0, "rmate", mate)
     settle(1, "rmate", mate)
-    spread(3)
     settle(0, "rfar", far)
     finish(2)
     settle(0, "ron", cross)
@@ -319,7 +329,7 @@
     return pl.pallas_call(
         kernel,
         out_shape=pltpu.VMEM((OWN, RHS), BF16),
-        in_specs=[hbm] * 6,
+        in_specs=[hbm] * 4 + [pl.BlockSpec(memory_space=pltpu.VMEM), hbm],
         out_specs=pl.BlockSpec(memory_space=pltpu.VMEM),
         scratch_shapes=[
             pltpu.VMEM((OWN, RHS), BF16),
@@ -328,25 +338,25 @@
             pltpu.VMEM((OWN, PIECE), F32),
             pltpu.VMEM((PIECES, LEAF, PIECE), BF16),
             pltpu.VMEM((SENT, OWN, PIECE), BF16),
-            pltpu.VMEM((LEAF, PIECE), BF16),
+            pltpu.VMEM((LEAF, SENT * PIECE), BF16),
             pltpu.VMEM((LEAF, LEAF), BF16),
             pltpu.VMEM((LEAF, LEVELS * RANK), BF16),
             pltpu.VMEM((LEVELS * RANK, LEAF), BF16),
             pltpu.VMEM((LEVELS, 1, RANK, RANK), F32),
-            pltpu.SMEM((1,), jnp.int32),
             pltpu.VMEM((LEAF, PIECE), BF16),
-            pltpu.VMEM((PIECES, LEAF, PIECE), F32),
+            pltpu.VMEM((LEAF, SENT * PIECE), F32),
+            pltpu.VMEM((CHIP, KEPT * PIECE), F32),
             pltpu.VMEM((PIECES, LEAF, PIECE), BF16),
             pltpu.VMEM((SENT, OWN, PIECE), BF16),
             pltpu.VMEM((PIECES, 3, RANK, PIECE), BF16),
             pltpu.VMEM((PIECES, 3, RANK, PIECE), BF16),
-            pltpu.VMEM((LAST, 3, PART, PIECE), BF16),
-            pltpu.VMEM((LAST, 3, PART, PIECE), BF16),
-            pltpu.VMEM((LAST, RANK, PIECE), F32),
+            pltpu.VMEM((PIECES, 3, PART, PIECE), BF16),
+            pltpu.VMEM((PIECES, 3, PART, PIECE), BF16),
+            pltpu.VMEM((PIECES, RANK, PIECE), F32),
             pltpu.VMEM((PIECES, RANK, PIECE), BF16),
             pltpu.VMEM((PIECES, RANK, PIECE), BF16),
-            pltpu.VMEM((LAST, RANK, PIECE), BF16),
-            pltpu.VMEM((3, RANK, PIECE), BF16),
+            pltpu.VMEM((PIECES, RANK, PIECE), BF16),
+            pltpu.VMEM((PIECES, 3, RANK, PIECE), BF16),
             dma((12,)),
             dma((COPIES * PIECES,)),
             dma((COPIES * PIECES,)),
@@ -360,7 +370,7 @@
         name="operator",
     )(
         *(pltpu.with_memory_space_constraint(array, pltpu.HBM) for array in arrays[:4]),
-        arrays[4],
+        jnp.broadcast_to(arrays[4], (8, PIECE)),
         pltpu.with_memory_space_constraint(arrays[5], pltpu.HBM),
     )
 

time: 46.3 us -> 45.4 us (0.981)
  Pallas kernels: 44.4 us -> 43.4 us
    pallas_call x1, Pallas kernels: 44.4 us -> 43.4 us  [on_device(): pl.pallas_call(kernel, out_shape=pltpu.VMEM((OWN, RHS), BF16), in_specs=[...]
where the time goes in v4:
time: 45.4 us; the launch traced here: 45.2 us
  Pallas kernels  43.4 us (96%)
  local copies, waits for them, and re-layouts  1.15 us (3%)
  between operations  0.67 us (1%)
    pallas_call x1, Pallas kernels, on_device(): pl.pallas_call(kernel, out_shape=pltpu.VMEM((OWN, RHS), BF16), in_specs=[...  43.4 us
    unnamed x1, local copies, waits for them, and re-layouts  1.15 us

profile of v4, /device:TPU:1, one launch (start us, length us, event | category | flops | bytes accessed | tf_op | source)
XLA Modules:
  0.0 45.2 jit_solution(12390741669669454998)
XLA Ops:
  0.7 43.4 %operator.1 = bf16[512,1536]{1,0:T(8,128)(2,1)S(1)} custom-call(bf16[512,1536]{1,0:T(8,128)(2,1)} %x_hbm.1, bf16[2048,2048]{1,0:T(8,128)(2,1)} %near_hbm.1, bf16[3,2048,128]{2,1,0:T(8,128)(2,1)} %bases_hbm.1, f32[3,1,128,128]{3,2,1,0:T(8,128)} %core_hbm.1, s32[8,128]{1,0:T(8,128)S(1)} %broadcast_in_dim.2.rows, f32[512]{0:T(512)} %nugget_hbm.1), custom_call_target="tpu_custom_call" | custom-call | flops 4000000000 | bytes 15000000 | tf_op jit(solution)/shard_map/operator/pallas_call | solution.py:329
  44.1 1.1 %copy.8 = bf16[512,1536]{1,0:T(8,128)(2,1)} copy(bf16[512,1536]{1,0:T(8,128)(2,1)S(1)} %operator.1) | data formatting | bytes 3145728
  (1 shorter events, 0.0 us)

commit v5 on v4

--- a/solution.py
+++ b/solution.py
@@ -23,15 +23,15 @@
 RHS = 1536
 PART = 32
 BLOCK = 512
-CROSS = (3,)
+EARLY = PIECES - 1
 COPIES = 18
 
 
 def kernel(
     x_hbm, near_hbm, bases_hbm, core_hbm, rows, nugget_hbm, out,
     own, noise, scale, live, xs, relay, xm, near, bases, bases_t, core, mask, total, total_kept, result, back,
-    out0, in0, out1, in1, sum2, out2, in2, sib2, in3,
-    local_sem, send_sem, recv_sem,
+    out0, in0, out1, in1, sum2, out2, in2, sib2, mine_half, out_half, in_half,
+    local_sem, send_sem, recv_sem, ready,
 ):
     leaf = lax.axis_index("leaf")
     rhs = lax.axis_index("rhs")
@@ -47,8 +47,17 @@
     to_pair = (leaf + 4 - 8 * x_lo, rhs)
 
     barrier = pltpu.get_barrier_semaphore()
-    for device in (to_far, to_pair, *to_ys, to_mate):
+    for device in (to_far, to_mate):
         pl.semaphore_signal(barrier, inc=1, device_id=device, device_id_type=MESH)
+    for j in range(3):
+
+        @pl.when(ys[j] > y)
+        def _():
+            pl.semaphore_signal(barrier, inc=1, device_id=to_ys[j], device_id_type=MESH)
+
+    @pl.when(x_lo == 0)
+    def _():
+        pl.semaphore_signal(barrier, inc=1, device_id=to_pair, device_id_type=MESH)
 
     def rows_of(index):
         return pl.ds(pl.multiple_of(index * OWN, OWN), OWN)
@@ -94,19 +103,13 @@
         c["far"] = remote(at + 2, x_hbm.at[:, cols_of(far, k)], xs.at[k, rows_of(rhs)], to_far)
         c["on"] = remote(at + 3, passed, xs.at[k, rows_of(mate)], to_far)
         c["zero"] = [remote(at + 4 + j, out0.at[k, j], in0.at[k, j], to_ys[j]) for j in range(3)]
-        if k not in CROSS:
-            first = pl.ds(0, PART)
-            c["one"] = [
-                remote(at + 7 + j, out1.at[k, j], in1.at[k, j], to_ys[j]) for j in range(3)
-            ]
-            c["two"] = remote(at + 10, out2.at[k, first], in2.at[k, first], to_pair)
-            c["three"] = [
-                remote(at + 11 + j, in2.at[k, first], sib2.at[k, part_of(y)], to_ys[j])
-                for j in range(3)
-            ]
-        else:
-            c["two"] = remote(at + 10, out2.at[k], in2.at[k], to_pair)
-            c["three"] = [remote(at + 11 + j, in2.at[k], in3.at[k, j], to_ys[j]) for j in range(3)]
+        c["one"] = [remote(at + 7 + j, out1.at[k, j], in1.at[k, j], to_ys[j]) for j in range(3)]
+        c["two"] = remote(at + 10, out2.at[k], in2.at[k], to_pair)
+        c["three"] = [
+            remote(at + 11 + j, in2.at[k], sib2.at[k, part_of(y)], to_ys[j]) for j in range(3)
+        ]
+        if k == EARLY:
+            c["half"] = remote(at + 14, out_half, in_half, to_far)
         mine = out.at[:, cols_of(rhs, k)]
         if k < SENT:
             c["rfar"] = remote(at + 14, result.at[k, rows_of(far)], mine, to_far)
@@ -117,7 +120,7 @@
 
     every = [copies(k) for k in range(PIECES)]
 
-    pl.semaphore_wait(barrier, 6)
+    pl.semaphore_wait(barrier, 2 + y + x_lo)
 
     every[0]["relay"].start()
     every[0]["far"].start()
@@ -128,6 +131,15 @@
     own_x = [load(x_hbm.at[:, cols_of(rhs, k)], xs.at[k, rows_of(rhs)]) for k in range(PIECES)]
     for k in range(1, PIECES):
         every[k]["mate"].start()
+    for j in range(3):
+
+        @pl.when(ys[j] < y)
+        def _():
+            pl.semaphore_signal(ready, inc=1, device_id=to_ys[j], device_id_type=MESH)
+
+    @pl.when(x_lo == 1)
+    def _():
+        pl.semaphore_signal(ready, inc=1, device_id=to_pair, device_id_type=MESH)
 
     count = rows[0:1, :]
 
@@ -177,22 +189,25 @@
         cols = cols_of(which, k)
         add_noise(cols, out[:, cols])
 
+    def send_parts(k, part):
+        sum2[k] = part
+        for j in range(3):
+            out1[k, j] = sum2[k, part_of(ys[j])].astype(BF16)
+            every[k]["one"][j].start()
+
     def gather(k):
         c = every[k]
-        own_x[k].wait()
+        if k != EARLY:
+            own_x[k].wait()
         if k < SENT:
             c["mate"].wait_recv()
         c["far"].wait_recv()
         c["on"].wait_recv()
-        part = jnp.dot(bases_t[...], xs[k], preferred_element_type=F32)
-        if k not in CROSS:
-            sum2[k] = part[2 * RANK :]
-            for j in range(3):
-                out1[k, j] = sum2[k, part_of(ys[j])].astype(BF16)
-                c["one"][j].start()
+        if k == EARLY:
+            part = jnp.dot(bases_t[: 2 * RANK], xs[k], preferred_element_type=F32)
         else:
-            out2[k] = part[2 * RANK :].astype(BF16)
-            c["two"].start()
+            part = jnp.dot(bases_t[...], xs[k], preferred_element_type=F32)
+            send_parts(k, part[2 * RANK :])
         middle = part[RANK : 2 * RANK].astype(BF16)
         out0[k, 0] = part[:RANK].astype(BF16)
         out0[k, 1] = middle
@@ -219,37 +234,52 @@
         at = (k - SENT) * PIECE
         return total_kept[rows_of(owner % 2), at : at + PIECE]
 
-    def exchange(k):
-        c = every[k]
+    def quarter(k):
         part = sum2[k, part_of(y)]
         for j in range(3):
-            c["one"][j].wait_recv()
+            every[k]["one"][j].wait_recv()
             part = part + in1[k, j].astype(F32)
-        out2[k, :PART] = part.astype(BF16)
-        c["two"].start()
+        return part
+
+    def exchange(k):
+        out2[k] = quarter(k).astype(BF16)
+        every[k]["two"].start()
+
+    def early_parts():
+        own_x[EARLY].wait()
+        every[EARLY]["mate"].wait_recv()
+        at = pl.ds(pl.multiple_of((rhs // 2) * CHIP, CHIP), CHIP)
+        send_parts(
+            EARLY,
+            jnp.dot(bases_t[2 * RANK :, at], xs[EARLY, at], preferred_element_type=F32),
+        )
+
+    def early_half():
+        part = quarter(EARLY)
+        mine_half[...] = part
+        out_half[...] = part.astype(BF16)
+        every[EARLY]["half"].start()
+
+    def early_exchange():
+        every[EARLY]["half"].wait_recv()
+        out2[EARLY] = (mine_half[...] + in_half[...].astype(F32)).astype(BF16)
+        every[EARLY]["two"].start()
 
     def spread(k):
         c = every[k]
         c["two"].wait_recv()
         for copy in c["three"]:
             copy.start()
-        if k not in CROSS:
-            sib2[k, part_of(y)] = in2[k, :PART]
+        sib2[k, part_of(y)] = in2[k]
 
     def finish(k):
         c = every[k]
         for copy in c["zero"] + c["three"]:
             copy.wait_recv()
-        if k not in CROSS:
-            top = sib2[k].astype(F32)
-        else:
-            top = in2[k].astype(F32)
-            for j in range(3):
-                top = top + in3[k, j].astype(F32)
         sibling = (
             in0[k, 0].astype(F32),
             in0[k, 1].astype(F32) + in0[k, 2].astype(F32),
-            top,
+            sib2[k].astype(F32),
         )
         mapped = jnp.concatenate(
             [
@@ -275,10 +305,17 @@
         value = near_of(k, rhs) + jnp.dot(bases[at, :], mapped, preferred_element_type=F32)
         add_noise(cols_of(rhs, k), value.astype(BF16))
 
+
+    @pl.when(y + x_lo < 4)
+    def _():
+        pl.semaphore_wait(ready, 4 - y - x_lo)
+
+    early_parts()
     gather(0)
     load_near.wait()
     load_core.wait()
     load_own.wait()
+    early_half()
     exchange(0)
     every[2]["mate"].wait_recv()
     every[2]["on"].start()
@@ -287,39 +324,39 @@
     spread(0)
     near_sent(0)
     near_sent(1)
+    early_exchange()
     exchange(1)
-    every[3]["mate"].wait_recv()
     every[3]["on"].start()
     gather(2)
     finish(0)
     spread(1)
     exchange(2)
-    gather(3)
     every[0]["back"].wait_recv()
     every[0]["ron"].start()
+    spread(3)
+    gather(3)
     finish(1)
     spread(2)
     every[1]["back"].wait_recv()
     every[1]["ron"].start()
-    spread(3)
     near_kept()
+    finish(3)
     settle(0, "rmate", mate)
     settle(1, "rmate", mate)
     settle(0, "rfar", far)
     finish(2)
     settle(0, "ron", cross)
-    finish(3)
+    settle(3, "rmate", mate)
     settle(2, "rmate", mate)
     settle(1, "rfar", far)
-    settle(3, "rmate", mate)
     settle(1, "ron", cross)
 
     for k in range(PIECES):
         c = every[k]
-        for name in ("relay", "mate", "far", "on", "two", "rfar", "back", "rmate", "ron"):
+        for name in ("relay", "mate", "far", "on", "half", "two", "rfar", "back", "rmate", "ron"):
             if name in c:
                 c[name].wait_send()
-        for copy in c["zero"] + c.get("one", []) + c["three"]:
+        for copy in c["zero"] + c["one"] + c["three"]:
             copy.wait_send()
 
 
@@ -353,13 +390,16 @@
             pltpu.VMEM((PIECES, 3, PART, PIECE), BF16),
             pltpu.VMEM((PIECES, 3, PART, PIECE), BF16),
             pltpu.VMEM((PIECES, RANK, PIECE), F32),
+            pltpu.VMEM((PIECES, PART, PIECE), BF16),
+            pltpu.VMEM((PIECES, PART, PIECE), BF16),
             pltpu.VMEM((PIECES, RANK, PIECE), BF16),
-            pltpu.VMEM((PIECES, RANK, PIECE), BF16),
-            pltpu.VMEM((PIECES, RANK, PIECE), BF16),
-            pltpu.VMEM((PIECES, 3, RANK, PIECE), BF16),
+            pltpu.VMEM((PART, PIECE), F32),
+            pltpu.VMEM((PART, PIECE), BF16),
+            pltpu.VMEM((PART, PIECE), BF16),
             dma((12,)),
             dma((COPIES * PIECES,)),
             dma((COPIES * PIECES,)),
+            pltpu.SemaphoreType.REGULAR,
         ],
         compiler_params=pltpu.CompilerParams(
             collective_id=0, has_side_effects=True, vmem_limit_bytes=48 << 20

time: 45.4 us -> 43.6 us (0.960)
  Pallas kernels: 43.4 us -> 41.7 us
    pallas_call x1, Pallas kernels: 43.4 us -> 41.7 us  [on_device(): pl.pallas_call(kernel, out_shape=pltpu.VMEM((OWN, RHS), BF16), in_specs=[...]
where the time goes in v5:
time: 43.6 us; the launch traced here: 43.5 us
  Pallas kernels  41.7 us (96%)
  local copies, waits for them, and re-layouts  1.15 us (3%)
  between operations  0.67 us (2%)
    pallas_call x1, Pallas kernels, on_device(): pl.pallas_call(kernel, out_shape=pltpu.VMEM((OWN, RHS), BF16), in_specs=[...  41.7 us
    unnamed x1, local copies, waits for them, and re-layouts  1.15 us

profile of v5, /device:TPU:1, one launch (start us, length us, event | category | flops | bytes accessed | tf_op | source)
XLA Modules:
  0.0 43.5 jit_solution(14749652494511769905)
XLA Ops:
  0.7 41.7 %operator.1 = bf16[512,1536]{1,0:T(8,128)(2,1)S(1)} custom-call(bf16[512,1536]{1,0:T(8,128)(2,1)} %x_hbm.1, bf16[2048,2048]{1,0:T(8,128)(2,1)} %near_hbm.1, bf16[3,2048,128]{2,1,0:T(8,128)(2,1)} %bases_hbm.1, f32[3,1,128,128]{3,2,1,0:T(8,128)} %core_hbm.1, s32[8,128]{1,0:T(8,128)S(1)} %broadcast_in_dim.2.rows, f32[512]{0:T(512)} %nugget_hbm.1), custom_call_target="tpu_custom_call" | custom-call | flops 4000000000 | bytes 15000000 | tf_op jit(solution)/shard_map/operator/pallas_call | solution.py:366
  42.4 1.1 %copy.8 = bf16[512,1536]{1,0:T(8,128)(2,1)} copy(bf16[512,1536]{1,0:T(8,128)(2,1)S(1)} %operator.1) | data formatting | bytes 3145728
  (1 shorter events, 0.0 us)

commit v6 on v5

--- a/solution.py
+++ b/solution.py
@@ -29,7 +29,8 @@
 
 def kernel(
     x_hbm, near_hbm, bases_hbm, core_hbm, rows, nugget_hbm, out,
-    own, noise, scale, live, xs, relay, xm, near, bases, bases_t, core, mask, total, total_kept, result, back,
+    own, noise, scale, live, xs, relay, xm, near, bases, bases_t, core, mask,
+    total, total_kept, result, back,
     out0, in0, out1, in1, sum2, out2, in2, sib2, mine_half, out_half, in_half,
     local_sem, send_sem, recv_sem, ready,
 ):
@@ -79,11 +80,6 @@
         copy.start()
         local.append(copy)
         return copy
-
-    load_noise = load(nugget_hbm, noise)
-    load_bases = [
-        load(bases_hbm.at[l], bases.at[:, pl.ds(l * RANK, RANK)]) for l in range(LEVELS)
-    ]
 
     def remote(index, src, dst, device):
         return pltpu.make_async_remote_copy(
@@ -122,10 +118,14 @@
 
     pl.semaphore_wait(barrier, 2 + y + x_lo)
 
+    every[0]["far"].start()
     every[0]["relay"].start()
-    every[0]["far"].start()
     every[1]["relay"].start()
     every[0]["mate"].start()
+    load_noise = load(nugget_hbm, noise)
+    load_bases = [
+        load(bases_hbm.at[l], bases.at[:, pl.ds(l * RANK, RANK)]) for l in range(LEVELS)
+    ]
     every[0]["relay"].wait_recv()
     every[0]["on"].start()
     own_x = [load(x_hbm.at[:, cols_of(rhs, k)], xs.at[k, rows_of(rhs)]) for k in range(PIECES)]
@@ -293,7 +293,8 @@
         )
         owners = ((mate, "rmate"),)
         if k < SENT:
-            owners = ((far, "rfar"), (cross, "back")) + owners
+            first = ((far, "rfar"), (cross, "back"))
+            owners = (first[::-1] if k else first) + owners
         for owner, name in owners:
             at = rows_of(owner)
             value = near_of(k, owner) + jnp.dot(
@@ -304,7 +305,6 @@
         at = rows_of(rhs)
         value = near_of(k, rhs) + jnp.dot(bases[at, :], mapped, preferred_element_type=F32)
         add_noise(cols_of(rhs, k), value.astype(BF16))
-
 
     @pl.when(y + x_lo < 4)
     def _():
@@ -336,9 +336,9 @@
     spread(3)
     gather(3)
     finish(1)
-    spread(2)
     every[1]["back"].wait_recv()
     every[1]["ron"].start()
+    spread(2)
     near_kept()
     finish(3)
     settle(0, "rmate", mate)
@@ -348,16 +348,16 @@
     settle(0, "ron", cross)
     settle(3, "rmate", mate)
     settle(2, "rmate", mate)
-    settle(1, "rfar", far)
-    settle(1, "ron", cross)
-
     for k in range(PIECES):
         c = every[k]
         for name in ("relay", "mate", "far", "on", "half", "two", "rfar", "back", "rmate", "ron"):
-            if name in c:
+            if name in c and c[name] is not every[1]["ron"]:
                 c[name].wait_send()
         for copy in c["zero"] + c["one"] + c["three"]:
             copy.wait_send()
+    settle(1, "rfar", far)
+    settle(1, "ron", cross)
+    every[1]["ron"].wait_send()
 
 
 def on_device(*arrays):

time: 43.6 us -> 43.4 us (level)
  no operation moved by 1% of the time
where the time goes in v6:
time: 43.4 us; the launch traced here: 43.2 us
  Pallas kernels  41.4 us (95%)
  local copies, waits for them, and re-layouts  1.15 us (3%)
  between operations  0.67 us (2%)
    pallas_call x1, Pallas kernels, on_device(): pl.pallas_call(kernel, out_shape=pltpu.VMEM((OWN, RHS), BF16), in_specs=[...  41.4 us
    unnamed x1, local copies, waits for them, and re-layouts  1.15 us

profile of v6, /device:TPU:1, one launch (start us, length us, event | category | flops | bytes accessed | tf_op | source)
XLA Modules:
  0.0 43.2 jit_solution(14659807909107470667)
XLA Ops:
  0.7 41.4 %operator.1 = bf16[512,1536]{1,0:T(8,128)(2,1)S(1)} custom-call(bf16[512,1536]{1,0:T(8,128)(2,1)} %x_hbm.1, bf16[2048,2048]{1,0:T(8,128)(2,1)} %near_hbm.1, bf16[3,2048,128]{2,1,0:T(8,128)(2,1)} %bases_hbm.1, f32[3,1,128,128]{3,2,1,0:T(8,128)} %core_hbm.1, s32[8,128]{1,0:T(8,128)S(1)} %broadcast_in_dim.2.rows, f32[512]{0:T(512)} %nugget_hbm.1), custom_call_target="tpu_custom_call" | custom-call | flops 4000000000 | bytes 15000000 | tf_op jit(solution)/shard_map/operator/pallas_call | solution.py:366
  42.1 1.1 %copy.8 = bf16[512,1536]{1,0:T(8,128)(2,1)} copy(bf16[512,1536]{1,0:T(8,128)(2,1)S(1)} %operator.1) | data formatting | bytes 3145728
  (1 shorter events, 0.0 us)

commit v7 on v6

--- a/solution.py
+++ b/solution.py
@@ -324,8 +324,8 @@
     spread(0)
     near_sent(0)
     near_sent(1)
+    exchange(1)
     early_exchange()
-    exchange(1)
     every[3]["on"].start()
     gather(2)
     finish(0)
@@ -333,8 +333,8 @@
     exchange(2)
     every[0]["back"].wait_recv()
     every[0]["ron"].start()
+    gather(3)
     spread(3)
-    gather(3)
     finish(1)
     every[1]["back"].wait_recv()
     every[1]["ron"].start()

time: 43.4 us -> 43.4 us (level)
  no operation moved by 1% of the time
where the time goes in v7:
time: 43.4 us; the launch traced here: 43.3 us
  Pallas kernels  41.5 us (96%)
  local copies, waits for them, and re-layouts  1.15 us (3%)
  between operations  0.67 us (2%)
    pallas_call x1, Pallas kernels, on_device(): pl.pallas_call(kernel, out_shape=pltpu.VMEM((OWN, RHS), BF16), in_specs=[...  41.5 us
    unnamed x1, local copies, waits for them, and re-layouts  1.15 us

profile of v7, /device:TPU:1, one launch (start us, length us, event | category | flops | bytes accessed | tf_op | source)
XLA Modules:
  0.0 43.3 jit_solution(3548210048209202502)
XLA Ops:
  0.7 41.5 %operator.1 = bf16[512,1536]{1,0:T(8,128)(2,1)S(1)} custom-call(bf16[512,1536]{1,0:T(8,128)(2,1)} %x_hbm.1, bf16[2048,2048]{1,0:T(8,128)(2,1)} %near_hbm.1, bf16[3,2048,128]{2,1,0:T(8,128)(2,1)} %bases_hbm.1, f32[3,1,128,128]{3,2,1,0:T(8,128)} %core_hbm.1, s32[8,128]{1,0:T(8,128)S(1)} %broadcast_in_dim.2.rows, f32[512]{0:T(512)} %nugget_hbm.1), custom_call_target="tpu_custom_call" | custom-call | flops 4000000000 | bytes 15000000 | tf_op jit(solution)/shard_map/operator/pallas_call | solution.py:366
  42.1 1.1 %copy.8 = bf16[512,1536]{1,0:T(8,128)(2,1)} copy(bf16[512,1536]{1,0:T(8,128)(2,1)S(1)} %operator.1) | data formatting | bytes 3145728
  (1 shorter events, 0.0 us)
